TPU v7x, 32 devices: a whole 2x2x4 slice. The times are simulated.
32 devices in a mesh: seq: 2 (over y), blk: 16 (over z, x, core).
Axes of the slice: x: 2, y: 2, z: 4, core: 2. Of those that a mesh axis runs over, the one named last changes fastest.
Arguments:
- hidden: bfloat16 [2, 4096, 768], P('seq', 'blk'), may hold values from -6 to 6
- positions: int32 [2, 4096], P('seq', 'blk'), may hold values from 0 to 4095, as said below
- ln_attn_gain: bfloat16 [768], replicated, may hold values from 0.099609375 to 1.8984375
- ln_attn_bias: bfloat16 [768], replicated, may hold values from -4 to 4
- ln_mlp_gain: bfloat16 [768], replicated, may hold values from 0.099609375 to 1.8984375
- ln_mlp_bias: bfloat16 [768], replicated, may hold values from -4 to 4
- w_qkv: bfloat16 [768, 2304], replicated, may hold values from -0.21875 to 0.21875
- b_qkv: bfloat16 [2304], replicated, may hold values from -4 to 4
- w_dense: bfloat16 [768, 768], replicated, may hold values from -1.75 to 1.75
- b_dense: bfloat16 [768], replicated, may hold values from -4 to 4
- w_in: bfloat16 [768, 3072], replicated, may hold values from -0.21875 to 0.21875
- b_in: bfloat16 [3072], replicated, may hold values from -6 to 6
- w_out: bfloat16 [3072, 768], replicated, may hold values from -0.15625 to 0.15625
- b_out: bfloat16 [768], replicated, may hold values from -4 to 4
- out_grad: bfloat16 [2, 4096, 768], P('seq', 'blk'), may hold values from -6 to 6
Outputs:
- output: bfloat16 [2, 4096, 768], P('seq', 'blk')
- input_grad: bfloat16 [2, 4096, 768], P('seq', 'blk')
- ln_attn_gain_grad: float32 [768], replicated
- ln_attn_bias_grad: float32 [768], replicated
- ln_mlp_gain_grad: float32 [768], replicated
- ln_mlp_bias_grad: float32 [768], replicated
- w_qkv_grad: float32 [768, 2304], replicated
- b_qkv_grad: float32 [2304], replicated
- w_dense_grad: float32 [768, 768], replicated
- b_dense_grad: float32 [768], replicated
- w_in_grad: float32 [768, 3072], replicated
- b_in_grad: float32 [3072], replicated
- w_out_grad: float32 [3072, 768], replicated
- b_out_grad: float32 [768], replicated
Inputs may be any that keep to these rules, and one draw needn't show every extreme that they name: In each sequence the positions are a permutation of 0 to 4095; the 256 rows of one device hold two runs of 128 consecutive positions, group c and group 32 - 1 - c for some c.
All inputs are finite; a program needn't handle non-finite values.
Results may differ from a plain program's by a relative error of at most 0.0093.
Values may be sent and summed in bfloat16 or wider, within the bound.
A program may use at most 384 MiB of HBM per device.

v0:
```python
import functools

import jax
import jax.numpy as jnp
import numpy as np
from jax import lax
from jax.experimental import pallas as pl
from jax.experimental.pallas import tpu as pltpu
from jax.sharding import PartitionSpec as P

HEADS = 12
HEAD_DIM = 64
ROTARY = 16
GROUP = 128
HEAD_GROUPS = 4
PER_GROUP = HEADS // HEAD_GROUPS
NORM_EPSILON = 1e-05
ROTARY_BASE = 10000.0
MASKED = -1e30
VMEM_BYTES = 62 * 1024 * 1024

F32 = jnp.float32
BF16 = jnp.bfloat16
IN_VMEM = pl.BlockSpec(memory_space=pltpu.VMEM)
IN_SMEM = pl.BlockSpec(memory_space=pltpu.SMEM)


def mm(a, b):
    return lax.dot_general(a, b, (((1,), (0,)), ((), ())), preferred_element_type=F32)


def mm_nt(a, b):
    return lax.dot_general(a, b, (((1,), (1,)), ((), ())), preferred_element_type=F32)


def mm_tn(a, b):
    return lax.dot_general(a, b, (((0,), (0,)), ((), ())), preferred_element_type=F32)


def normalise(rows):
    centre = rows - jnp.mean(rows, axis=-1, keepdims=True)
    spread = jnp.mean(centre * centre, axis=-1, keepdims=True)
    scale = lax.rsqrt(spread + NORM_EPSILON)
    return centre * scale, scale


def norm_back(grad, xhat, scale, gain):
    eg = grad * gain
    return scale * (
        eg
        - jnp.mean(eg, axis=-1, keepdims=True)
        - xhat * jnp.mean(eg * xhat, axis=-1, keepdims=True)
    )


def params():
    return pltpu.CompilerParams(vmem_limit_bytes=VMEM_BYTES)


def front_kernel(hid, og, gain, bias, wqkv, bqkv, wdense, cosw, sina, sinb, msg):
    rows = hid[...].astype(F32)
    xhat, _ = normalise(rows)
    normed = (xhat * gain[...].astype(F32) + bias[...].astype(F32)).astype(BF16)
    mixed = mm(normed, wqkv[...]) + bqkv[...].astype(F32)
    datt = mm_nt(og[...], wdense[...])
    width = hid.shape[1]
    lane = lax.broadcasted_iota(jnp.int32, (rows.shape[0], 128), 1)
    low = lane < HEAD_DIM
    ca, sa, sb = cosw[...], sina[...], sinb[...]

    def turned(u):
        return u * ca + pltpu.roll(u, 120, 1) * sa + pltpu.roll(u, 8, 1) * sb

    for tile in range(HEADS // 2):
        at = tile * 128
        q = turned(mixed[:, at : at + 128]) * (HEAD_DIM**-0.5)
        k = turned(mixed[:, width + at : width + at + 128])
        v = mixed[:, 2 * width + at : 2 * width + at + 128]
        d = datt[:, at : at + 128]
        for part, (one, two) in enumerate(((q, d), (k, v))):
            for odd in range(2):
                head = 2 * tile + odd
                if odd == 0:
                    packed = jnp.where(low, one, pltpu.roll(two, 64, 1))
                else:
                    packed = jnp.where(low, pltpu.roll(one, 64, 1), two)
                msg[head % PER_GROUP, head // PER_GROUP, part] = packed.astype(BF16)


def front(hid, og, gain, bias, wqkv, bqkv, wdense, tables):
    rows = hid.shape[0]
    return pl.pallas_call(
        front_kernel,
        out_shape=jax.ShapeDtypeStruct((PER_GROUP, HEAD_GROUPS, 2, rows, 128), BF16),
        in_specs=[IN_VMEM] * 10,
        out_specs=IN_VMEM,
        compiler_params=params(),
        name="front",
    )(hid, og, gain, bias, wqkv, bqkv, wdense, *tables)


def mlp_kernel(
    core, hid, og, again, abias, mgain, mbias, win, bin_, wout,
    grads, bin_grad, out_part, gn_part, normed_attn, normed_s,
):
    step = pl.program_id(0)

    @pl.when(step == 0)
    def _():
        xhat, _ = normalise(hid[...].astype(F32))
        normed_s[...] = (xhat * mgain[...].astype(F32) + mbias[...].astype(F32)).astype(BF16)
        normed_attn[...] = (xhat * again[...].astype(F32) + abias[...].astype(F32)).astype(BF16)
        out_part[...] = jnp.zeros_like(out_part)
        gn_part[...] = jnp.zeros_like(gn_part)

    x = normed_s[...]
    w1 = win[...]
    w2 = wout[...]
    inner = mm(x, w1) + bin_[...].astype(F32)
    cdf = 0.5 * (1.0 + lax.erf(inner * (0.5**0.5)))
    act = (inner * cdf).astype(BF16)
    pdf = jnp.exp(-0.5 * inner * inner) * (0.5 * 2.0**0.5 * 3.141592653589793**-0.5)
    gact = mm_nt(og[...], w2)
    ginner = (gact * (cdf + inner * pdf)).astype(BF16)
    bin_grad[...] = jnp.sum(ginner.astype(F32), axis=0, keepdims=True)
    grads[0] = mm_tn(ginner, x).astype(BF16)
    grads[1] = mm_tn(act, og[...]).astype(BF16)
    out_part[...] += mm(act, w2)
    gn_part[...] += mm_nt(ginner, w1)


def mlp(core, hid, og, again, abias, mgain, mbias, win, b_in, wout):
    rows, width = hid.shape
    half = win.shape[1] // 2
    chunk = 512
    steps = half // chunk
    whole = lambda i, c: (0, 0)
    return pl.pallas_call(
        mlp_kernel,
        grid_spec=pltpu.PrefetchScalarGridSpec(
            num_scalar_prefetch=1,
            grid=(steps,),
            in_specs=[
                pl.BlockSpec((rows, width), whole),
                pl.BlockSpec((rows, width), whole),
                pl.BlockSpec((1, width), whole),
                pl.BlockSpec((1, width), whole),
                pl.BlockSpec((1, width), whole),
                pl.BlockSpec((1, width), whole),
                pl.BlockSpec((width, chunk), lambda i, c: (0, c[0] * steps + i)),
                pl.BlockSpec((1, chunk), lambda i, c: (0, c[0] * steps + i)),
                pl.BlockSpec((chunk, width), lambda i, c: (c[0] * steps + i, 0)),
            ],
            out_specs=[
                pl.BlockSpec((2, chunk, width), lambda i, c: (0, i, 0)),
                pl.BlockSpec((1, chunk), lambda i, c: (0, i)),
                pl.BlockSpec((rows, width), whole),
                pl.BlockSpec((rows, width), whole),
                pl.BlockSpec((rows, width), whole),
            ],
            scratch_shapes=[pltpu.VMEM((rows, width), BF16)],
        ),
        out_shape=[
            jax.ShapeDtypeStruct((2, half, width), BF16),
            jax.ShapeDtypeStruct((1, half), F32),
            jax.ShapeDtypeStruct((rows, width), F32),
            jax.ShapeDtypeStruct((rows, width), F32),
            jax.ShapeDtypeStruct((rows, width), BF16),
        ],
        compiler_params=params(),
        name="mlp",
    )(core, hid, og, again, abias, mgain, mbias, win, b_in, wout)


def attention_kernel(blocks, pieces, n_query, *refs):
    tab = refs[0]
    qd_ref = refs[1]
    kv_refs = refs[2 : 2 + pieces]
    odq_ref = refs[2 + pieces]
    dkv_refs = refs[3 + pieces : 3 + 2 * pieces]
    kvs, kvt, sbuf, acc = refs[3 + 2 * pieces :]
    kb_rows = blocks
    per_piece = kv_refs[0].shape[0]
    n_run = pieces * per_piece

    def group_rows(g):
        return pl.ds(pl.multiple_of(g * GROUP, GROUP), GROUP)

    for piece in range(pieces):

        def place(i, _, piece=piece):
            rows = group_rows(tab[piece * per_piece + i])
            blk = kv_refs[piece][i]
            kvs[rows, :] = blk
            kvt[:, rows] = blk.T
            acc[rows, :] = jnp.zeros((GROUP, 128), F32)
            return 0

        lax.fori_loop(0, per_piece, place, 0, unroll=4)

    lane = lax.broadcasted_iota(jnp.int32, (2 * GROUP, 128), 1)
    row = lax.broadcasted_iota(jnp.int32, (128, 2 * GROUP), 0)
    qcol = lax.broadcasted_iota(jnp.int32, (1, 2 * GROUP), 1)
    krow = lax.broadcasted_iota(jnp.int32, (kb_rows, 1), 0)

    def pair_step(pair, _):
        i0 = tab[n_run + 2 * pair]
        i1 = tab[n_run + 2 * pair + 1]
        g0 = tab[n_run + n_query + 2 * pair]
        g1 = tab[n_run + n_query + 2 * pair + 1]
        qd = jnp.concatenate([qd_ref[i0], qd_ref[i1]], axis=0)
        zero = jnp.zeros_like(qd)
        w_keys = jnp.concatenate(
            [jnp.where(lane < HEAD_DIM, qd, zero), jnp.where(lane >= HEAD_DIM, qd, zero)], axis=0
        )
        qdt = qd.T
        zero_t = jnp.zeros_like(qdt)
        w_score = jnp.where(row < HEAD_DIM, qdt, zero_t)
        w_dprob = jnp.where(row >= HEAD_DIM, qdt, zero_t)
        qpos = jnp.where(qcol < GROUP, g0 * GROUP + qcol, (g1 - 1) * GROUP + qcol)
        n_full = (g0 * GROUP) // kb_rows
        n_all = (g1 * GROUP) // kb_rows + 1

        def block_rows(kb):
            return pl.ds(pl.multiple_of(kb * kb_rows, kb_rows), kb_rows)

        def score_step(kb, top, masked):
            rows = block_rows(kb)
            s = mm(kvs[rows, :], w_score)
            if masked:
                s = jnp.where(kb * kb_rows + krow <= qpos, s, MASKED)
            sbuf[rows, :] = s
            return jnp.maximum(top, jnp.max(s.reshape(kb_rows // 8, 8, 2 * GROUP), axis=0))

        top = jnp.full((8, 2 * GROUP), MASKED, F32)
        top = lax.fori_loop(0, n_full, lambda kb, c: score_step(kb, c, False), top)
        top = lax.fori_loop(n_full, n_all, lambda kb, c: score_step(kb, c, True), top)
        top = jnp.max(top, axis=0, keepdims=True)

        def value_step(kb, carry):
            total, out = carry
            rows = block_rows(kb)
            e = jnp.exp(sbuf[rows, :] - top)
            sbuf[rows, :] = e
            total = total + jnp.sum(e.reshape(kb_rows // 8, 8, 2 * GROUP), axis=0)
            return total, out + mm(kvt[HEAD_DIM:128, rows], e.astype(BF16))

        total, out = lax.fori_loop(
            0,
            n_all,
            value_step,
            (jnp.zeros((8, 2 * GROUP), F32), jnp.zeros((HEAD_DIM, 2 * GROUP), F32)),
        )
        inv = 1.0 / jnp.sum(total, axis=0, keepdims=True)
        out = out * inv
        delta = jnp.sum(out * qdt[HEAD_DIM:128, :].astype(F32), axis=0, keepdims=True)

        def grad_step(kb, dq):
            rows = block_rows(kb)
            p = sbuf[rows, :] * inv
            dp = mm(kvs[rows, :], w_dprob)
            ds = (p * (dp - delta)).astype(BF16)
            acc[rows, :] += mm(jnp.concatenate([ds, p.astype(BF16)], axis=1), w_keys)
            return dq + mm(kvt[0:HEAD_DIM, rows], ds)

        dq = lax.fori_loop(0, n_all, grad_step, jnp.zeros((HEAD_DIM, 2 * GROUP), F32))
        odq = jnp.concatenate([out, dq * (HEAD_DIM**-0.5)], axis=0).astype(BF16).T
        odq_ref[i0] = odq[:GROUP]
        odq_ref[i1] = odq[GROUP:]
        return 0

    lax.fori_loop(0, n_query // 2, pair_step, 0)

    for piece in range(pieces):

        def give(i, _, piece=piece):
            dkv_refs[piece][i] = acc[group_rows(tab[piece * per_piece + i]), :].astype(BF16)
            return 0

        lax.fori_loop(0, per_piece, give, 0, unroll=4)


def attention(tab, qd, kvs):
    pieces = len(kvs)
    n_query = qd.shape[0]
    n_key = pieces * kvs[0].shape[0] * GROUP
    blocks = 1024
    run = jax.ShapeDtypeStruct(kvs[0].shape, BF16)
    outs = pl.pallas_call(
        functools.partial(attention_kernel, blocks, pieces, n_query),
        out_shape=[jax.ShapeDtypeStruct(qd.shape, BF16)] + [run] * pieces,
        in_specs=[IN_SMEM] + [IN_VMEM] * (1 + pieces),
        out_specs=[IN_VMEM] * (1 + pieces),
        scratch_shapes=[
            pltpu.VMEM((n_key, 128), BF16),
            pltpu.VMEM((128, n_key), BF16),
            pltpu.VMEM((n_key, 2 * GROUP), F32),
            pltpu.VMEM((n_key, 128), F32),
        ],
        compiler_params=params(),
        name="attention",
    )(tab, qd, *kvs)
    return outs[0], outs[1:]


class Place:
    def __init__(self, n_seq, n_blk):
        self.n_seq, self.n_blk = n_seq, n_blk
        self.n_low = n_blk // HEAD_GROUPS
        self.n_rest = n_blk // 4
        self.s = lax.axis_index("seq")
        self.b = lax.axis_index("blk")
        self.core = self.b % 2
        self.x = (self.b // 2) % 2
        self.rest = self.b // 4
        self.hi = self.b // self.n_low

    def flip(self, bit):
        step = 1 << bit
        return (self.s, self.b + step - 2 * step * ((self.b // step) % 2))

    def to_seq(self):
        return ((self.s + 1) % self.n_seq, self.b)

    def to_rest(self, by):
        return (self.s, ((self.rest + by) % self.n_rest) * 4 + self.b % 4)

    def to_group(self, by):
        return (self.s, ((self.hi + by) % HEAD_GROUPS) * self.n_low + self.b % self.n_low)

    def partners(self):
        found = [self.flip(bit) for bit in range(self.n_low.bit_length() - 1)]
        found += [self.to_seq()]
        found += [self.to_rest(by) for by in range(1, self.n_rest)]
        if self.n_low != 4:
            found += [self.to_group(by) for by in range(1, HEAD_GROUPS)]
        return found

    def meet(self):
        barrier = pltpu.get_barrier_semaphore()
        partners = self.partners()
        for device in partners:
            pl.semaphore_signal(
                barrier, inc=1, device_id=device, device_id_type=pl.DeviceIdType.MESH
            )
        pl.semaphore_wait(barrier, len(partners))


class Wires:
    def __init__(self, sends, recvs):
        self.sends, self.recvs, self.used = sends, recvs, 0

    def copy(self, src, dst, device):
        at = self.used
        self.used += 1
        return pltpu.make_async_remote_copy(
            src_ref=src,
            dst_ref=dst,
            send_sem=self.sends.at[at],
            recv_sem=self.recvs.at[at],
            device_id=device,
            device_id_type=pl.DeviceIdType.MESH,
        )


def add_rows(dst, dst_at, others, count, out=None, out_at=0, lanes=slice(None), got_lanes=slice(None)):
    block = 16
    for size in (96, 64, 48, 32):
        if count % size == 0:
            block = size
            break
    out = dst if out is None else out

    def step(i, _):
        total = dst[pl.ds(pl.multiple_of(dst_at + i * block, 16), block), lanes].astype(F32)
        for ref, start in others:
            rows = pl.ds(pl.multiple_of(start + i * block, 16), block)
            total = total + ref[rows, got_lanes].astype(F32)
        out[pl.ds(pl.multiple_of(out_at + i * block, 16), block), lanes] = total.astype(BF16)
        return 0

    lax.fori_loop(0, count // block, step, 0)


def unit_copies(n_rest):
    return 2 * (2 + n_rest - 1) + 1


class Unit:
    def __init__(self, place, wires, data, base, size, order, got1, got2, got3, out, final, final_base, local):
        pairs = {"x": (place.x, place.flip(1)), "y": (place.s, place.to_seq())}
        (self.bit1, self.dev1), (self.bit2, self.dev2) = pairs[order[0]], pairs[order[1]]
        self.place, self.data, self.out = place, data, out
        self.base, self.size = base, size
        self.h, self.q = size // 2, size // 4
        n = place.n_rest
        self.cuts = 1 if (self.q // n) % 16 == 0 else 2
        self.e = self.q * self.cuts // n
        self.w = data.shape[1] // self.cuts
        self.base1 = base + self.bit1 * self.h
        self.base2 = self.base1 + self.bit2 * self.q
        self.got1, self.got2, self.got3 = got1, got2, got3
        self.fetch = None
        if local is not None:
            kept = pl.ds(pl.multiple_of(self.base1, 16), self.h)
            self.fetch = pltpu.make_async_copy(data.at[kept], out.at[kept], local)
        z = place.rest

        def cell(ref, start, index):
            at = pl.multiple_of(start + (index // self.cuts) * self.e, 16)
            if self.cuts == 1:
                return ref.at[pl.ds(at, self.e)]
            return ref.at[
                pl.ds(at, self.e), pl.ds(pl.multiple_of((index % self.cuts) * self.w, 128), self.w)
            ]

        def landing(by):
            slot = pl.ds((by - 1) * self.e, self.e)
            return got3.at[slot] if self.cuts == 1 else got3.at[slot, pl.ds(0, self.w)]

        def rows(ref, start, count):
            return ref.at[pl.ds(pl.multiple_of(start, 16), count)]

        self.rs1 = [wires.copy(rows(data, base + (1 - self.bit1) * self.h, self.h), got1, self.dev1)]
        self.rs2 = [wires.copy(rows(got1, (1 - self.bit2) * self.q, self.q), got2, self.dev2)]
        self.rs3 = [
            wires.copy(cell(got2, 0, (z + by) % n), landing(by), place.to_rest(by))
            for by in range(1, n)
        ]
        self.ag3 = [
            wires.copy(cell(out, self.base2, z), cell(out, self.base2, z), place.to_rest(by))
            for by in range(1, n)
        ]
        self.ag2 = [wires.copy(rows(out, self.base2, self.q), rows(out, self.base2, self.q), self.dev2)]
        self.ag1 = [wires.copy(rows(out, self.base1, self.h), rows(out, self.base1, self.h), self.dev1)]
        self.agc = [
            wires.copy(
                rows(out, base, size),
                final.at[place.core, pl.ds(final_base, size)],
                place.flip(0),
            )
        ]
        self.sent = []

    def start(self, copies):
        for copy in copies:
            copy.start()
        self.sent = self.sent + copies

    def arrive(self, copies):
        for copy in copies:
            copy.wait_recv()

    def stage0(self):
        self.start(self.rs1)
        if self.fetch is not None:
            self.fetch.start()

    def stage1(self):
        self.arrive(self.rs1)
        for copy in self.rs1:
            copy.wait_send()
        self.sent = [copy for copy in self.sent if not any(copy is gone for gone in self.rs1)]
        if self.fetch is not None:
            self.fetch.wait()
        add_rows(self.got1, 0, [(self.data if self.fetch is None else self.out, self.base1)], self.h)
        self.start(self.rs2)

    def stage2(self):
        self.arrive(self.rs2)
        add_rows(self.got2, 0, [(self.got1, self.bit2 * self.q)], self.q)
        self.start(self.rs3)

    def stage3(self):
        self.arrive(self.rs3)
        others = [(self.got3, k * self.e) for k in range(self.place.n_rest - 1)]
        z = self.place.rest
        at = (z // self.cuts) * self.e
        lanes = got_lanes = slice(None)
        if self.cuts > 1:
            lanes = pl.ds(pl.multiple_of((z % self.cuts) * self.w, 128), self.w)
            got_lanes = pl.ds(0, self.w)
        add_rows(self.got2, at, others, self.e, self.out, self.base2 + at, lanes, got_lanes)
        self.start(self.ag3)

    def stage4(self):
        self.arrive(self.ag3)
        self.start(self.ag2)

    def stage5(self):
        self.arrive(self.ag2)
        self.start(self.ag1)

    def stage6(self):
        self.arrive(self.ag1)
        self.start(self.agc)

    def finish(self):
        self.arrive(self.agc)
        for copy in self.sent:
            copy.wait_send()


def tail_compute(
    odq, dkv, hi, hid, og, again, mgain, wqkv, wdense, bdense, bout, mout, gnm,
    cosw, sina, sinb, output, input_grad, send, small,
):
    rows = hid[...].astype(F32)
    count, width = rows.shape
    lane = lax.broadcasted_iota(jnp.int32, (count, 128), 1)
    low = lane < HEAD_DIM
    ca, sa, sb = cosw[...], sina[...], sinb[...]

    def turned_back(g):
        return g * ca - pltpu.roll(g, 120, 1) * sa - pltpu.roll(g, 8, 1) * sb

    def head(ref, a):
        at = (a // PER_GROUP - hi + HEAD_GROUPS) % HEAD_GROUPS
        return ref[a % PER_GROUP, at].astype(F32)

    outs, grads = [], [[], [], []]
    for tile in range(HEADS // 2):
        one, two = head(odq, 2 * tile), head(odq, 2 * tile + 1)
        outs.append(jnp.where(low, one, pltpu.roll(two, 64, 1)).astype(BF16))
        grads[0].append(turned_back(jnp.where(low, pltpu.roll(one, 64, 1), two)).astype(BF16))
        one, two = head(dkv, 2 * tile), head(dkv, 2 * tile + 1)
        grads[1].append(
            turned_back(jnp.where(low, one, pltpu.roll(two, 64, 1))).astype(BF16)
        )
        grads[2].append(jnp.where(low, pltpu.roll(one, 64, 1), two).astype(BF16))
    att = jnp.concatenate(outs, axis=1)
    dmixed = jnp.concatenate(grads[0] + grads[1] + grads[2], axis=1)
    half_m, half_a = dmixed.shape[1] // 2, width // 2
    for side in range(2):
        send[side, :, :half_m] = dmixed[:, side * half_m : (side + 1) * half_m]
        send[side, :, half_m:] = att[:, side * half_a : (side + 1) * half_a]
    branch = mm(att, wdense[...]) + bdense[...].astype(F32)
    output[...] = (rows + branch + (mout + bout[...].astype(F32))).astype(BF16)
    gna = mm_nt(dmixed, wqkv[...])
    xhat, scale = normalise(rows)
    cot = og[...].astype(F32)
    input_grad[...] = (
        cot
        + norm_back(gna, xhat, scale, again[...].astype(F32))
        + norm_back(gnm, xhat, scale, mgain[...].astype(F32))
    ).astype(BF16)
    small[0:1, :] = jnp.sum(gna * xhat, axis=0, keepdims=True)
    small[1:2, :] = jnp.sum(gna, axis=0, keepdims=True)
    small[2:3, :] = jnp.sum(gnm * xhat, axis=0, keepdims=True)
    small[3:4, :] = jnp.sum(gnm, axis=0, keepdims=True)
    for part in range(3):
        cols = dmixed[:, part * width : (part + 1) * width].astype(F32)
        small[4 + part : 5 + part, :] = jnp.sum(cols, axis=0, keepdims=True)
    small[7:8, :] = jnp.sum(cot, axis=0, keepdims=True)


def weight_compute(own, other, normed, og, grads):
    half_m = own.shape[1] * 3 // 4
    both = jnp.concatenate([own, other], axis=0)
    grads[0:half_m, :] = mm_tn(both[:, :half_m], normed[...]).astype(BF16)
    grads[half_m:, :] = mm_tn(both[:, half_m:], og[...]).astype(BF16)


def finish_kernel(
    n_seq, n_blk, units1, units2, pieces,
    odq0, odq1, odq2, *refs,
):
    dkvs = [refs[j * pieces : (j + 1) * pieces] for j in range(PER_GROUP)]
    (
        grads1, out_part, gn_part, hid, og, og2, normed2, bins, again, mgain, wqkv, wdense, bdense, bout,
        cosw, sina, sinb,
        output, input_grad, small_out, final,
        odq_all, dkv_all, dkv_got, mout_got, gn_got, send, other, grads2, small, small_got,
        got1, got2, got3, out1, out2, sends, recvs, local_sem,
    ) = refs[PER_GROUP * pieces :]
    place = Place(n_seq, n_blk)
    wires = Wires(sends, recvs)
    odqs = (odq0, odq1, odq2)
    tokens, width = hid.shape
    n_rest = place.n_rest
    rows1 = grads1.shape[0]
    place.meet()
    sent = []

    def go(copy):
        copy.start()
        sent.append(copy)
        return copy

    mout_copy = go(wires.copy(out_part.at[pl.ds(tokens, tokens)], mout_got, place.flip(0)))
    gn_copy = go(wires.copy(gn_part.at[pl.ds(tokens, tokens)], gn_got, place.flip(0)))
    low_bits = place.n_low.bit_length() - 1
    stage_copies = []
    for j in range(PER_GROUP):
        half = pieces // 2
        stage_copies.append([
            go(wires.copy(dkvs[j][half + i], dkv_got.at[j, i], place.flip(0))) for i in range(half)
        ])
    home = []
    for j in range(PER_GROUP):
        for by in range(1, HEAD_GROUPS):
            home.append(go(wires.copy(odqs[j].at[by], odq_all.at[j, by], place.to_group(HEAD_GROUPS - by))))
    units = []
    at = 0
    for base, size, order in units1:
        units.append(Unit(
            place, wires, grads1, base, size, order,
            got1.at[pl.ds(at // 2, size // 2)], got2.at[pl.ds(at // 4, size // 4)],
            got3.at[pl.ds(at // 2, size // 2)], out1, final, base, local_sem.at[2 + len(units)],
        ))
        at += size
    units_b = []
    for base, size, order in units2:
        units_b.append(Unit(
            place, wires, grads2, base, size, order,
            got1.at[pl.ds(at // 2, size // 2)], got2.at[pl.ds(at // 4, size // 4)],
            got3.at[pl.ds(at // 2, size // 2)], out2, final, rows1 + base, None,
        ))
        at += size
    for unit in units:
        unit.stage0()

    slot = 0
    half = pieces // 2
    for bit in range(low_bits):
        after = slot + half
        for j in range(PER_GROUP):
            for copy in stage_copies[j]:
                copy.wait_recv()
            for i in range(half):
                mine = dkvs[j][i][...] if bit == 0 else dkv_got[j, slot - 2 * half + i]
                dkv_got[j, slot + i] = (mine.astype(F32) + dkv_got[j, slot + i].astype(F32)).astype(BF16)
            if half > 1:
                stage_copies[j] = [
                    go(wires.copy(dkv_got.at[j, slot + half // 2 + i], dkv_got.at[j, after + i], place.flip(bit + 1)))
                    for i in range(half // 2)
                ]
            else:
                for by in range(1, HEAD_GROUPS):
                    home.append(go(wires.copy(
                        dkv_got.at[j, slot, by], dkv_all.at[j, by], place.to_group(HEAD_GROUPS - by)
                    )))
                dkv_all[j, 0] = dkv_got[j, slot, 0]
        slot = after
        half //= 2
    for j in range(PER_GROUP):
        odq_all[j, 0] = odqs[j][0]
    for unit in units:
        unit.stage1()
    for copy in home:
        copy.wait_recv()
    mout_copy.wait_recv()
    gn_copy.wait_recv()
    mout = out_part[0:tokens, :] + mout_got[...]
    gnm = gn_part[0:tokens, :] + gn_got[...]
    tail_compute(
        odq_all, dkv_all, place.hi, hid, og, again, mgain, wqkv, wdense, bdense, bout, mout, gnm,
        cosw, sina, sinb, output, input_grad, send, small,
    )
    other_copy = go(wires.copy(send.at[1 - place.core], other, place.flip(0)))
    for unit in units:
        unit.stage2()
    other_copy.wait_recv()
    weight_compute(send[place.core], other[...], normed2, og2, grads2)
    for unit in units_b:
        unit.stage0()
    small[8:, :] = bins[...]
    for unit in units:
        unit.stage3()
    for unit in units_b:
        unit.stage1()
    order = [[place.flip(0)], [place.flip(1)], [place.to_seq()], [place.to_rest(by) for by in range(1, n_rest)]]
    slot = 0
    for devices in order:
        copies = [wires.copy(small, small_got.at[slot + i], device) for i, device in enumerate(devices)]
        for copy in copies:
            copy.start()
        for copy in copies:
            copy.wait()
        total = small[...]
        for i in range(len(devices)):
            total = total + small_got[slot + i]
        small[...] = total
        slot += len(devices)
    small_out[...] = small[...]
    for unit in units:
        unit.stage4()
    for unit in units_b:
        unit.stage2()
    for unit in units:
        unit.stage5()
    for unit in units_b:
        unit.stage3()
    for unit in units:
        unit.stage6()
    for unit in units_b:
        unit.stage4()
    for unit in units_b:
        unit.stage5()
    for unit in units_b:
        unit.stage6()
    keep1 = pltpu.make_async_copy(out1, final.at[place.core, pl.ds(0, rows1)], local_sem.at[0])
    keep2 = pltpu.make_async_copy(out2, final.at[place.core, pl.ds(rows1, grads2.shape[0])], local_sem.at[1])
    keep1.start()
    keep2.start()
    for unit in units + units_b:
        unit.finish()
    for copy in sent:
        copy.wait_send()
    keep1.wait()
    keep2.wait()


def finish(mesh, odqs, dkvs, grads1, out_part, gn_part, hid, og, og2, normed2, bins, again, mgain, wqkv, wdense, bdense, bout, tables):
    n_seq, n_blk = mesh.shape["seq"], mesh.shape["blk"]
    n_rest = n_blk // 4
    tokens, width = hid.shape
    pieces = len(dkvs[0])
    rows1, rows2 = grads1.shape[0], 2 * width
    fine = (rows1 // 4) % (4 * n_rest * 16) == 0
    parts = 4 if fine else 2
    units1 = [(i * rows1 // parts, rows1 // parts, "xy" if 2 * i < parts else "yx") for i in range(parts)]
    parts = 2 if fine else 1
    units2 = [(i * rows2 // parts, rows2 // parts, "xy" if 2 * i < parts else "yx") for i in range(parts)]
    total = rows1 + rows2
    copies = (len(units1) + len(units2)) * unit_copies(n_rest)
    copies += 3 + PER_GROUP * (2 * (HEAD_GROUPS - 1) + pieces - 1) + 3 + n_rest - 1
    line = (HEAD_GROUPS, tokens, 128)
    n_small = 8 + bins.shape[0]
    inputs = list(odqs) + [p for d in dkvs for p in d] + [
        grads1, out_part, gn_part, hid, og, og2, normed2, bins, again, mgain, wqkv, wdense, bdense, bout, *tables,
    ]
    return pl.pallas_call(
        functools.partial(finish_kernel, n_seq, n_blk, units1, units2, pieces),
        out_shape=[
            jax.ShapeDtypeStruct((tokens, width), BF16),
            jax.ShapeDtypeStruct((tokens, width), BF16),
            jax.ShapeDtypeStruct((n_small, width), F32),
            jax.ShapeDtypeStruct((2, total, width), BF16),
        ],
        in_specs=[pl.BlockSpec(memory_space=pl.ANY) if v is grads1 else IN_VMEM for v in inputs],
        out_specs=[IN_VMEM] * 3 + [pl.BlockSpec(memory_space=pl.ANY)],
        scratch_shapes=[
            pltpu.VMEM((PER_GROUP,) + line, BF16),
            pltpu.VMEM((PER_GROUP,) + line, BF16),
            pltpu.VMEM((PER_GROUP, pieces - 1) + line, BF16),
            pltpu.VMEM((tokens, width), F32),
            pltpu.VMEM((tokens, width), F32),
            pltpu.VMEM((2, tokens, 2 * width), BF16),
            pltpu.VMEM((tokens, 2 * width), BF16),
            pltpu.VMEM((rows2, width), BF16),
            pltpu.VMEM((n_small, width), F32),
            pltpu.VMEM((3 + n_rest - 1, n_small, width), F32),
            pltpu.VMEM((total // 2, width), BF16),
            pltpu.VMEM((total // 4, width), BF16),
            pltpu.VMEM((total // 2, width), BF16),
            pltpu.VMEM((rows1, width), BF16),
            pltpu.VMEM((rows2, width), BF16),
            pltpu.SemaphoreType.DMA((copies,)),
            pltpu.SemaphoreType.DMA((copies,)),
            pltpu.SemaphoreType.DMA((2 + len(units1),)),
        ],
        compiler_params=pltpu.CompilerParams(
            vmem_limit_bytes=VMEM_BYTES, collective_id=1, has_side_effects=True
        ),
        name="finish",
    )(*inputs)


def expand_kernel(marks, block, *outs):
    step = pl.program_id(0)
    for out, (first, last, turn) in zip(outs, marks):

        @pl.when((step >= first) & (step < last))
        def _(out=out, turn=turn):
            rows = block[0].astype(F32)
            out[...] = rows.T if turn else rows


def expand(final, sizes):
    width = final.shape[2]
    block = width // 2
    marks, specs, shapes, firsts = [], [], [], []
    first = offset = 0
    for rows, turn in sizes:
        each = rows // block
        marks.append((first, first + 2 * each, turn))
        firsts.append((first, each, offset))

        def at(i, first=first, count=2 * each):
            return jnp.clip(i - first, 0, count - 1)

        if turn:
            specs.append(pl.BlockSpec((width, block), lambda i, at=at: (0, at(i))))
            shapes.append(jax.ShapeDtypeStruct((width, 2 * rows), F32))
        else:
            specs.append(pl.BlockSpec((block, width), lambda i, at=at: (at(i), 0)))
            shapes.append(jax.ShapeDtypeStruct((2 * rows, width), F32))
        first += 2 * each
        offset += each

    def source(i):
        core, row = 0, 0
        for begin, each, offset in firsts:
            here = (i >= begin) & (i < begin + 2 * each)
            core = jnp.where(here, (i - begin) // each, core)
            row = jnp.where(here, offset + (i - begin) % each, row)
        return (core, row, 0)

    return pl.pallas_call(
        functools.partial(expand_kernel, marks),
        grid=(first,),
        in_specs=[pl.BlockSpec((1, block, width), source)],
        out_specs=specs,
        out_shape=shapes,
        compiler_params=params(),
        name="expand",
    )(final)


def half_rows(d):
    return pl.ds(pl.multiple_of(d * GROUP, GROUP), GROUP)


class Attention:
    def __init__(self, lines, devices, flags, kk, vv, kkt, vvt, sb, acc):
        self.lines, self.devices, self.flags = lines, devices, flags
        self.kk, self.vv, self.kkt, self.vvt = kk, vv, kkt, vvt
        self.sb, self.acc = sb, acc
        self.n = devices * GROUP

    def prepare(self, pieces):
        low_lanes = lax.broadcasted_iota(jnp.int32, (GROUP, 128), 1) < HEAD_DIM
        for p, ref in enumerate(pieces):

            def step(r, _, p=p, ref=ref):
                rows = half_rows(p * self.lines + r)
                low, high = ref[r, 0:GROUP, :], ref[r, GROUP : 2 * GROUP, :]
                lowt, hight = low.T, high.T
                low, high = low.astype(F32), high.astype(F32)
                self.kk[rows, :] = jnp.where(low_lanes, low, pltpu.roll(high, 64, 1)).astype(BF16)
                self.vv[rows, :] = jnp.where(low_lanes, pltpu.roll(low, 64, 1), high).astype(BF16)
                self.kkt[0:HEAD_DIM, rows] = lowt[0:HEAD_DIM]
                self.kkt[HEAD_DIM:128, rows] = hight[0:HEAD_DIM]
                self.vvt[0:HEAD_DIM, rows] = lowt[HEAD_DIM:128]
                self.vvt[HEAD_DIM:128, rows] = hight[HEAD_DIM:128]
                self.acc[0, rows, :] = jnp.zeros((GROUP, 128), F32)
                self.acc[1, rows, :] = jnp.zeros((GROUP, 128), F32)
                return 0

            lax.fori_loop(0, self.lines, step, 0, unroll=self.lines)

    def masks(self, i):
        all_flags = self.flags[...].reshape(self.devices, 16, 128)
        mine = all_flags[i : i + 1]
        one, nil = jnp.ones(mine.shape, BF16), jnp.zeros(mine.shape, BF16)
        low, high = [], []
        for d in range(self.devices):
            theirs = all_flags[d : d + 1]
            low.append(one if d == i else jnp.where(theirs < mine, one, nil))
            high.append(nil if d == i else jnp.where(theirs > mine, one, nil))
        return jnp.concatenate(low + [nil], axis=0), jnp.concatenate(high + [one], axis=0)

    def pair(self, first, qd_ref, odq_ref):
        n, blocks = self.n, self.devices + 1
        wide = 2 * GROUP
        lane = lax.broadcasted_iota(jnp.int32, (GROUP, 128), 1)
        krow = lax.broadcasted_iota(jnp.int32, (GROUP, wide), 0)
        qcol = lax.broadcasted_iota(jnp.int32, (GROUP, wide), 1)
        seen = krow <= qcol % GROUP
        sb, kk, vv = self.sb, self.kk, self.vv
        masks, low_t, high_t, keys_w, both_w = [], [], [], [], []
        for slot in range(2):
            masks.append(self.masks(first + slot))
            qd = qd_ref[first + slot]
            qdt = qd.T
            low_t.append(qdt[:, 0:GROUP])
            high_t.append(qdt[:, GROUP:wide])
            low, high = qd[0:GROUP], qd[GROUP:wide]
            zero = jnp.zeros_like(low)
            ql, qh = jnp.where(lane < HEAD_DIM, low, zero), jnp.where(lane < HEAD_DIM, high, zero)
            dl, dh = jnp.where(lane < HEAD_DIM, zero, low), jnp.where(lane < HEAD_DIM, zero, high)
            keys_w.append(jnp.concatenate([jnp.concatenate([ql, qh], axis=1), jnp.concatenate([dl, dh], axis=1)], axis=0))
            both_w.append((qh, dh))
        none = jnp.zeros((128, GROUP), BF16)

        def diagonal(rows):
            own = [jnp.concatenate([low_t[k][rows], high_t[k][rows]], axis=0) for k in range(2)]
            return jnp.concatenate(
                [jnp.concatenate([own[0], none], axis=1), jnp.concatenate([none, own[1]], axis=1)], axis=0
            )

        def highs(rows):
            got = jnp.concatenate([high_t[0][rows], high_t[1][rows]], axis=1)
            return jnp.concatenate([got, jnp.zeros_like(got)], axis=0)

        q_rows, d_rows = slice(0, HEAD_DIM), slice(HEAD_DIM, 128)
        w_score, w_dprob = diagonal(q_rows), diagonal(d_rows)
        h_score, h_dprob = highs(q_rows), highs(d_rows)
        dout_low = jnp.concatenate([low_t[0][d_rows], low_t[1][d_rows]], axis=1).astype(F32)
        dout_high = jnp.concatenate([high_t[0][d_rows], high_t[1][d_rows]], axis=1).astype(F32)
        weights_all = jnp.concatenate([both_w[0][0], both_w[1][0], both_w[0][1], both_w[1][1]], axis=0)
        less = jnp.concatenate([low.astype(F32)[:, 0:8] for low, _ in masks], axis=2)
        low_lanes = lax.broadcasted_iota(jnp.int32, (blocks, 16, 128), 2) < HEAD_DIM

        def rows_seen(held):
            found = []
            for slot, (low, high) in enumerate(masks):
                lanes = jnp.where(low_lanes, low.astype(F32), high.astype(F32)).astype(BF16)
                x = jnp.concatenate([held[...], held[half_rows(first + slot), :]], axis=0)
                x = x.reshape(blocks, GROUP // 16, 16, 128) * lanes[:, None]
                found.append(x.reshape(blocks * GROUP, 128))
            return jnp.concatenate(found, axis=1)

        def columns_seen(held):
            found = []
            for slot, pair in enumerate(masks):
                for half, mask in enumerate(pair):
                    rows = slice(half * HEAD_DIM, half * HEAD_DIM + HEAD_DIM)
                    x = jnp.concatenate([held[rows, :], held[rows, half_rows(first + slot)]], axis=1)
                    line = jnp.concatenate([mask[d] for d in range(blocks)], axis=1)
                    x = x.reshape(HEAD_DIM // 16, 16, blocks * GROUP) * line[None]
                    found.append(x.reshape(HEAD_DIM, blocks * GROUP))
            return jnp.concatenate(found, axis=0)

        own, rest = pl.ds(0, blocks * GROUP), pl.ds(blocks * GROUP, n)

        def cut(x):
            return x.reshape(x.shape[0] // GROUP, GROUP // 8, 8, wide)

        def spread(low, high):
            return jnp.where(less > 0, low, high)[:, None]

        s = cut(mm(rows_seen(kk), w_score))
        hide = cut(jnp.where(seen, 0.0, MASKED))
        left = cut(jnp.where(seen | (qcol >= GROUP), 0.0, MASKED))
        right = cut(jnp.where(seen | (qcol < GROUP), 0.0, MASKED))
        s = [s[:first], s[first : first + 1] + left, s[first + 1 : first + 2] + right, s[first + 2 : -1], s[blocks - 1 :] + hide]
        s = jnp.concatenate([x for x in s if x.shape[0]], axis=0)
        sb[own, :] = s.reshape(blocks * GROUP, wide)
        tops = jnp.max(s, axis=1)
        s = mm(kk[...], h_score)
        sb[rest, :] = s
        top_low = jnp.max(jnp.max(jnp.where(less > 0, tops, MASKED), axis=0), axis=0, keepdims=True)
        top_high = jnp.maximum(
            jnp.max(jnp.where(less > 0, MASKED, tops), axis=0), jnp.max(s.reshape(n // 8, 8, wide), axis=0)
        )
        top_high = jnp.max(top_high, axis=0, keepdims=True)

        e = jnp.exp(cut(sb[own, :]) - spread(top_low, top_high))
        sums = jnp.sum(e, axis=1)
        e = e.reshape(blocks * GROUP, wide)
        sb[own, :] = e
        out = mm(columns_seen(self.vvt), e.astype(BF16))
        e = jnp.exp(sb[rest, :] - top_high)
        sb[rest, :] = e
        out_high = mm(self.vvt[0:HEAD_DIM, :], e.astype(BF16))
        total_low = jnp.sum(jnp.sum(jnp.where(less > 0, sums, 0.0), axis=0), axis=0, keepdims=True)
        total_high = jnp.sum(jnp.where(less > 0, 0.0, sums), axis=0) + jnp.sum(e.reshape(n // 8, 8, wide), axis=0)
        total_high = jnp.sum(total_high, axis=0, keepdims=True)

        def parts(x):
            low = jnp.concatenate([x[0:64, 0:GROUP], x[128:192, GROUP:wide]], axis=1)
            high = jnp.concatenate([x[64:128, 0:GROUP], x[192:256, GROUP:wide]], axis=1)
            return low, high

        yield
        inv_low, inv_high = 1.0 / total_low, 1.0 / total_high
        out_low, more = parts(out)
        out_low, out_high = out_low * inv_low, (out_high + more) * inv_high
        delta_low = jnp.sum(out_low * dout_low, axis=0, keepdims=True)
        delta_high = jnp.sum(out_high * dout_high, axis=0, keepdims=True)

        p = cut(sb[own, :]) * spread(inv_low, inv_high)
        dp = cut(mm(rows_seen(vv), w_dprob))
        ds = (p * (dp - spread(delta_low, delta_high))).reshape(blocks * GROUP, wide).astype(BF16)
        p = p.reshape(blocks * GROUP, wide).astype(BF16)
        dq = mm(columns_seen(self.kkt), ds)
        for slot in range(2):
            cols = slice(slot * GROUP, slot * GROUP + GROUP)
            got = mm(jnp.concatenate([ds[:, cols], p[:, cols]], axis=1), keys_w[slot])
            here = less[:, :, cols][:, None] > 0
            got = got.reshape(blocks, GROUP // 8, 8, wide)
            low = jnp.where(here, got[..., 0:128], 0.0).reshape(blocks * GROUP, 128)
            high = jnp.where(here, 0.0, got[..., 128:256]).reshape(blocks * GROUP, 128)
            self.acc[0] += low[0:n]
            self.acc[1] += high[0:n]
            self.acc[1, half_rows(first + slot), :] += high[n:]
        p = sb[rest, :] * inv_high
        dp = mm(vv[...], h_dprob)
        ds = (p * (dp - delta_high)).astype(BF16)
        self.acc[0] += mm(jnp.concatenate([ds, p.astype(BF16)], axis=1), weights_all)
        dq_low, dq_high = parts(dq)
        dq_high = dq_high + mm(self.kkt[0:HEAD_DIM, :], ds)
        for slot in range(2):
            cols = slice(slot * GROUP, slot * GROUP + GROUP)
            scale = HEAD_DIM**-0.5
            low = jnp.concatenate([out_low[:, cols], dq_low[:, cols] * scale], axis=0).astype(BF16).T
            high = jnp.concatenate([out_high[:, cols], dq_high[:, cols] * scale], axis=0).astype(BF16).T
            odq_ref[first + slot] = jnp.concatenate([low, high], axis=0)

    def give(self, dkv_refs):
        for p, ref in enumerate(dkv_refs):

            def step(r, _, p=p, ref=ref):
                rows = half_rows(p * self.lines + r)
                ref[r, 0:GROUP, :] = self.acc[0, rows, :].astype(BF16)
                ref[r, GROUP : 2 * GROUP, :] = self.acc[1, rows, :].astype(BF16)
                return 0

            lax.fori_loop(0, self.lines, step, 0, unroll=2)


def attention_scratch(lines, devices):
    n = devices * GROUP
    more = n + GROUP
    return [
        pltpu.VMEM((n, 128), BF16),
        pltpu.VMEM((n, 128), BF16),
        pltpu.VMEM((128, n), BF16),
        pltpu.VMEM((128, n), BF16),
        pltpu.VMEM((n + more, 256), F32),
        pltpu.VMEM((2, n, 128), F32),
    ]


class Chain:
    def __init__(self, place, wires, data, base, size, order, got, final, final_base, free, keep):
        pairs = {
            "x": (place.x, place.flip(1)),
            "y": (place.s, place.to_seq()),
            "m": (place.rest % 2, place.flip(2)),
            "f": (place.rest // 2, place.flip(3)),
        }
        self.data, self.got, self.sizes, self.bases, self.bits = data, [], [size], [base], []
        at = 0
        self.down, self.up = [], []
        for level, name in enumerate(order):
            bit, device = pairs[name]
            half = self.sizes[-1] // 2
            got_here = got.at[pl.ds(at, half)]
            at += half
            source, start = (data, base) if level == 0 else (self.got[-1], 0)
            away = pl.ds(pl.multiple_of(start + (1 - bit) * half, 16), half)
            self.down.append(wires.copy(source.at[away], got_here, device))
            self.got.append(got_here)
            self.bits.append(bit)
            self.sizes.append(half)
            self.bases.append(self.bases[-1] + bit * half)
            kept = pl.ds(pl.multiple_of(self.bases[-1], 16), half)
            self.up.append(wires.copy(data.at[kept], data.at[kept], device))
        whole = pl.ds(base, size)
        self.up.insert(0, wires.copy(data.at[whole], final.at[place.core, pl.ds(final_base, size)], place.flip(0)))
        self.depth = len(order)
        self.keep = pltpu.make_async_copy(data.at[whole], final.at[place.core, pl.ds(final_base, size)], keep)
        self.free, self.first = free, pairs[order[0]][1]
        self.sent = []

    def start(self, copy):
        copy.start()
        self.sent.append(copy)

    def stage(self, number):
        depth = self.depth
        if number == 0:
            self.start(self.down[0])
        elif number <= depth:
            level = number - 1
            self.down[level].wait_recv()
            if level == 0:
                self.down[0].wait_send()
                self.sent.pop()
                pl.semaphore_signal(
                    self.free, inc=1, device_id=self.first, device_id_type=pl.DeviceIdType.MESH
                )
            half = self.sizes[number]
            source, start = (self.data, self.bases[0]) if level == 0 else (self.got[level - 1], 0)
            start = start + self.bits[level] * half
            if number < depth:
                add_rows(self.got[level], 0, [(source, start)], half)
                self.start(self.down[number])
            else:
                add_rows(self.got[level], 0, [(source, start)], half, self.data, self.bases[depth])
                self.start(self.up[depth])
        else:
            level = 2 * depth - number + 1
            self.up[level].wait_recv()
            if level == 2:
                pl.semaphore_wait(self.free, 1)
            self.start(self.up[level - 1])
            if level == 1:
                self.keep.start()

    def finish(self):
        self.up[0].wait_recv()
        self.keep.wait()
        for copy in self.sent:
            copy.wait_send()


SCHEDULE = (
    "front", "send0", "mlp0", "u0.0", "u3.0", "mlp1", "mlp2", "u5.0", "send1", "line0", "spread0", "u0.1", "fwd0",
    "u4.0", "u3.1", "send2", "u5.1", "line1", "spread1", "keys0", "a0", "a0", "u0.2", "u4.1", "u5.2", "a0", "fwd1",
    "line2", "u3.2", "u0.3", "spread2", "u5.3", "a0", "u4.2", "u2.0", "keys1", "a1", "u5.4", "u3.3", "a1", "u1.0",
    "fwd2", "a1", "u0.4", "core0", "u5.5", "a1", "u2.1", "u5.6", "u3.4", "keys2", "a2", "u0.5", "core1", "a2",
    "plane0", "u1.1", "u4.3", "u5.7", "u0.6", "u3.5", "a2", "a2", "u2.2", "home0", "u3.6", "plane1", "u4.4", "u1.2",
    "core2", "grad0", "u0.7", "v0.1", "plane2", "home1", "u4.5", "u1.3", "grad1", "v0.2", "v1.1", "u2.3", "home2",
    "u4.6", "part", "u1.4", "v0.3", "v3.1", "v2.1", "u2.4", "grad2", "u1.5", "v0.4", "v3.2", "u4.7", "u1.6", "v0.5",
    "u3.7", "v2.2", "u2.5", "v3.3", "tail", "v4.1", "v3.4", "v5.1", "v2.3", "v0.6", "u2.6", "v1.2", "vec0", "u1.7",
    "v3.5", "v2.4", "u0.8", "v1.3", "v1.4", "u4.8", "u2.7", "v4.2", "u3.8", "v1.5", "v5.2", "v3.6", "v0.7", "v2.5",
    "v4.3", "v5.3", "u5.8", "v5.4", "v1.6", "v2.6", "v4.4", "v3.7", "u1.8", "v5.5", "v4.5", "v4.6", "v5.6", "v2.7",
    "vec1", "v0.8", "u2.8", "v4.7", "v5.7", "v1.7", "v3.8", "v2.8", "vec2", "v4.8", "v5.8", "vec3", "v1.8",
)
FF_CHUNK = 256
ORDERS = ("yxmf", "yxmf", "xymf", "xymf", "yxmf", "yxmf", "yxmf", "xymf", "yxmf", "xymf", "xymf", "yxmf")


def runs_of(positions, n_blk):
    group = positions[0, 0] // GROUP
    mirror = 2 * n_blk - 1 - group
    turn = jnp.full((16, 128), (group - mirror).astype(F32), F32).astype(BF16) > 0
    return jnp.minimum(group, mirror), jnp.broadcast_to(turn[None], (GROUP // 16, 16, 128))


def rotary_rows(low_group, n_blk):
    shape = (2 * GROUP, 2 * HEAD_DIM)
    row = lax.broadcasted_iota(jnp.int32, shape, 0)
    lane = lax.broadcasted_iota(jnp.int32, shape, 1) % HEAD_DIM
    half = ROTARY // 2
    at = jnp.where(row < GROUP, low_group * GROUP + row, (2 * n_blk - 2 - low_group) * GROUP + row)
    inverse = jnp.zeros(shape, F32)
    for i in range(half):
        inverse = jnp.where(lane % half == i, float(np.float32(ROTARY_BASE ** (-2.0 * i / ROTARY))), inverse)
    angles = at.astype(F32) * inverse
    cosine, sine = jnp.cos(angles), jnp.sin(angles)
    return (
        jnp.where(lane < ROTARY, cosine, 1.0),
        jnp.where(lane < half, -sine, 0.0),
        jnp.where((lane >= half) & (lane < ROTARY), sine, 0.0),
    )


def joined_kernel(
    n_seq, n_blk, units1, units2,
    positions, hid, og, again, abias, mgain, mbias, bqkv, bdense, bout, bin_,
    wqkv_hbm, wdense_hbm, win_hbm, wout_hbm,
    output, input_grad, vec_out, final,
    wqkv, wdense, win, wout, cosw, sina, sinb, hid2, og2, normed2, normed_m, qd_msg, kv_msg, qd_line, keys, flags,
    kk, vv, kkt, vvt, sb, acc,
    dkv_got, odq_all, dkv_all, out_part, gn_part, mout_got, gn_got, mine, other, bins,
    grads1, grads2, got, small, small_got, sends, recvs, load_sem, chunk_sem, keep_sem, free_sem,
):
    def row(ref):
        return ref[...].astype(F32).reshape(1, ref.shape[0])

    place = Place(n_seq, n_blk)
    wires = Wires(sends, recvs)
    tokens, width = hid.shape
    n_rest = place.n_rest
    core, hi = place.core, place.hi
    half_ff = win_hbm.shape[1] // 2
    chunks = half_ff // FF_CHUNK
    rows1 = grads1.shape[0]
    pieces = place.n_low
    sent, waiting = [], {}
    todo = {}

    def go(name, src, dst, device):
        copy = wires.copy(src, dst, device)
        copy.start()
        sent.append(copy)
        waiting.setdefault(name, []).append(copy)

    def arrive(name):
        for copy in waiting.pop(name):
            copy.wait_recv()

    loads = [
        pltpu.make_async_copy(wqkv_hbm, wqkv, load_sem.at[0]),
        pltpu.make_async_copy(wdense_hbm, wdense, load_sem.at[1]),
    ]
    for load in loads:
        load.start()

    def chunk_loads(f):
        slot = f % 2
        at = pl.multiple_of(core * half_ff + f * FF_CHUNK, FF_CHUNK)
        return [
            pltpu.make_async_copy(win_hbm.at[:, pl.ds(at, FF_CHUNK)], win.at[slot], chunk_sem.at[0, slot]),
            pltpu.make_async_copy(wout_hbm.at[pl.ds(at, FF_CHUNK), :], wout.at[slot], chunk_sem.at[1, slot]),
        ]

    for f in range(2):
        for load in chunk_loads(f):
            load.start()

    low_group, turned_rows = runs_of(positions, n_blk)
    cut = (GROUP // 16, 16, 128)
    for src, dst in ((hid, hid2), (og, og2)):
        for at in range(0, width, 128):
            cols = slice(at, at + 128)
            one, two = src[0:GROUP, cols].reshape(cut), src[GROUP : 2 * GROUP, cols].reshape(cut)
            dst[0:GROUP, cols] = jnp.where(turned_rows, two, one).reshape(GROUP, 128)
            dst[GROUP : 2 * GROUP, cols] = jnp.where(turned_rows, one, two).reshape(GROUP, 128)
    flags[0, 0] = jnp.full((16, 128), low_group.astype(F32), F32).astype(BF16)
    cosw[...], sina[...], sinb[...] = rotary_rows(low_group, n_blk)
    place.meet()
    for by in range(1, HEAD_GROUPS):
        go("flags", flags.at[0, 0], flags.at[0, by], place.to_group(by))
    for ref in (hid2, og2):
        go("rows", ref.at[pl.ds(0, tokens)], ref.at[pl.ds(tokens, tokens)], place.flip(0))

    lane = lax.broadcasted_iota(jnp.int32, (tokens, 128), 1)
    low = lane < HEAD_DIM

    def front():
        xhat, _ = normalise(hid2[0:tokens, :].astype(F32))
        normed = (xhat * row(again) + row(abias)).astype(BF16)
        for load in loads:
            load.wait()
        mixed = mm(normed, wqkv[...]) + row(bqkv)
        datt = mm_nt(og2[0:tokens, :], wdense[...])
        ca, sa, sb_ = cosw[...], sina[...], sinb[...]

        def turned(u):
            return u * ca + pltpu.roll(u, 120, 1) * sa + pltpu.roll(u, 8, 1) * sb_

        for tile in range(HEADS // 2):
            at = tile * 128
            q = turned(mixed[:, at : at + 128]) * (HEAD_DIM**-0.5)
            k = turned(mixed[:, width + at : width + at + 128])
            v = mixed[:, 2 * width + at : 2 * width + at + 128]
            d = datt[:, at : at + 128]
            for msg, one, two in ((qd_msg, q, d), (kv_msg, k, v)):
                for odd in range(2):
                    head = 2 * tile + odd
                    if odd == 0:
                        packed = jnp.where(low, one, pltpu.roll(two, 64, 1))
                    else:
                        packed = jnp.where(low, pltpu.roll(one, 64, 1), two)
                    msg[head % PER_GROUP, head // PER_GROUP] = packed.astype(BF16)
        arrive("flags")
        go("flag_x", flags.at[0], flags.at[1], place.flip(1))
        go("flag_c", flags.at[0], flags.at[2], place.flip(0))

    def send(j):
        for msg, line, name in ((kv_msg, keys.at[j, 0], "line"), (qd_msg, qd_line.at[j], "query")):
            for by in range(1, HEAD_GROUPS):
                go(name + str(j), msg.at[j, (hi + by) % HEAD_GROUPS], line.at[by], place.to_group(by))
        keys[j, 0, 0] = kv_msg[j, hi]
        qd_line[j, 0] = qd_msg[j, hi]

    def mlp_group(g):
        if g == 0:
            arrive("rows")
            xhat, _ = normalise(hid2[...].astype(F32))
            normed_m[...] = (xhat * row(mgain) + row(mbias)).astype(BF16)
            normed2[...] = (xhat * row(again) + row(abias)).astype(BF16)
            out_part[...] = jnp.zeros_like(out_part)
            gn_part[...] = jnp.zeros_like(gn_part)
        per = chunks // 3

        def step(f, _):
            slot = f % 2
            for load in chunk_loads(f):
                load.wait()
            x, w1, w2 = normed_m[...], win[slot], wout[slot]
            at = pl.multiple_of(f * FF_CHUNK, FF_CHUNK)
            bias_at = pl.ds(pl.multiple_of(core * half_ff + f * FF_CHUNK, FF_CHUNK), FF_CHUNK)
            inner = mm(x, w1) + bin_[bias_at].astype(F32).reshape(1, FF_CHUNK)
            cdf = 0.5 * (1.0 + lax.erf(inner * (0.5**0.5)))
            act = (inner * cdf).astype(BF16)
            pdf = jnp.exp(-0.5 * inner * inner) * (0.5 * 2.0**0.5 * 3.141592653589793**-0.5)
            gact = mm_nt(og2[...], w2)
            ginner = (gact * (cdf + inner * pdf)).astype(BF16)
            bins[0:1, pl.ds(at, FF_CHUNK)] = jnp.sum(ginner.astype(F32), axis=0, keepdims=True)
            grads1[pl.ds(at, FF_CHUNK), :] = mm_tn(ginner, x).astype(BF16)
            grads1[pl.ds(pl.multiple_of(half_ff + at, FF_CHUNK), FF_CHUNK), :] = mm_tn(act, og2[...]).astype(BF16)
            out_part[...] += mm(act, w2)
            gn_part[...] += mm_nt(ginner, w1)

            @pl.when(f + 2 < chunks)
            def _():
                for load in chunk_loads(f + 2):
                    load.start()

            return 0

        lax.fori_loop(g * per, (g + 1) * per, step, 0)

    def part():
        go("part", out_part.at[pl.ds(tokens, tokens)], mout_got, place.flip(0))
        go("part", gn_part.at[pl.ds(tokens, tokens)], gn_got, place.flip(0))

    def spread(j):
        go("x" + str(j), keys.at[j, 0], keys.at[j, 1], place.flip(1))
        go("c" + str(j), keys.at[j, 0], keys.at[j, 2], place.flip(0))

    def forward(j):
        arrive("x" + str(j))
        go("c" + str(j), keys.at[j, 1], keys.at[j, 3], place.flip(0))
        if j == 0:
            arrive("flag_x")
            go("flag_c", flags.at[1], flags.at[3], place.flip(0))

    def keys_there(j):
        arrive("c" + str(j))
        arrive("query" + str(j))
        if j == 0:
            arrive("flag_c")

    attention = Attention(HEAD_GROUPS, HEAD_GROUPS * pieces, flags, kk, vv, kkt, vvt, sb, acc)

    def attend(j):
        sources = [keys.at[j, p] for p in range(pieces)]
        attention.prepare(sources)
        for first in range(0, HEAD_GROUPS, 2):
            yield from attention.pair(first, qd_line.at[j], qd_line.at[j])
            if first + 2 < HEAD_GROUPS:
                yield
        for copy in leaving[j]:
            copy.wait_send()
        attention.give(sources)
        for by in range(1, HEAD_GROUPS):
            go("home" + str(j), qd_line.at[j, by], odq_all.at[j, by], place.to_group(HEAD_GROUPS - by))
        for i in range(2):
            go("core" + str(j), keys.at[j, 2 + i], dkv_got.at[j, i], place.flip(0))
        yield

    leaving = {}

    def core_sum(j):
        arrive("core" + str(j))
        for i in range(2):
            dkv_got[j, i] = (keys[j, i].astype(F32) + dkv_got[j, i].astype(F32)).astype(BF16)
        go("plane" + str(j), dkv_got.at[j, 1], dkv_got.at[j, 2], place.flip(1))

    def plane_sum(j):
        arrive("plane" + str(j))
        dkv_got[j, 2] = (dkv_got[j, 0].astype(F32) + dkv_got[j, 2].astype(F32)).astype(BF16)
        for by in range(1, HEAD_GROUPS):
            go("home" + str(j), dkv_got.at[j, 2, by], dkv_all.at[j, by], place.to_group(HEAD_GROUPS - by))
        odq_all[j, 0] = qd_line[j, 0]
        dkv_all[j, 0] = dkv_got[j, 2, 0]

    def home(j):
        arrive("home" + str(j))
        ca, sa, sb_ = cosw[...], sina[...], sinb[...]

        def turned_back(g):
            return g * ca - pltpu.roll(g, 120, 1) * sa - pltpu.roll(g, 8, 1) * sb_

        for g in range(HEAD_GROUPS):
            at = (g - hi + HEAD_GROUPS) % HEAD_GROUPS
            a, b = odq_all[j, at].astype(F32), dkv_all[j, at].astype(F32)
            mine[j, g, :, 0:128] = jnp.where(low, a, turned_back(a)).astype(BF16)
            mine[j, g, :, 128:256] = jnp.where(low, turned_back(b), b).astype(BF16)
        half = HEAD_GROUPS // 2
        go("other" + str(j), mine.at[j, pl.ds((1 - core) * half, half)], other.at[j], place.flip(0))

    def grad(j):
        arrive("other" + str(j))
        half = HEAD_GROUPS // 2
        normed, cot = normed2[...], og2[...]
        from_out = lax.broadcasted_iota(jnp.int32, (128, width), 0) < HEAD_DIM
        for g in range(half):
            both = jnp.concatenate([mine[j, core * half + g], other[j, g]], axis=0)
            base = (j * half + g) * 256
            by_normed = mm_tn(both, normed)
            by_cot = mm_tn(both[:, 0:128], cot)
            grads2[base : base + 128, :] = jnp.where(from_out, by_cot, by_normed[0:128]).astype(BF16)
            grads2[base + 128 : base + 256, :] = by_normed[128:256].astype(BF16)
        per = len(units2) // PER_GROUP
        for unit in second[j * per : (j + 1) * per]:
            unit.stage(0)

    def tail():
        arrive("part")
        rows = hid2[0:tokens, :].astype(F32)

        def parts(a):
            return mine[a % PER_GROUP, a // PER_GROUP].astype(F32)

        outs, grads = [], [[], [], []]
        for tile in range(HEADS // 2):
            one, two = parts(2 * tile), parts(2 * tile + 1)
            a1, b1, a2, b2 = one[:, 0:128], one[:, 128:256], two[:, 0:128], two[:, 128:256]
            outs.append(jnp.where(low, a1, pltpu.roll(a2, 64, 1)).astype(BF16))
            grads[0].append(jnp.where(low, pltpu.roll(a1, 64, 1), a2).astype(BF16))
            grads[1].append(jnp.where(low, b1, pltpu.roll(b2, 64, 1)).astype(BF16))
            grads[2].append(jnp.where(low, pltpu.roll(b1, 64, 1), b2).astype(BF16))
        att = jnp.concatenate(outs, axis=1)
        dmixed = jnp.concatenate(grads[0] + grads[1] + grads[2], axis=1)
        branch = mm(att, wdense[...]) + row(bdense)
        mout = out_part[0:tokens, :] + mout_got[...]
        output[...] = (rows + branch + (mout + row(bout))).astype(BF16)
        gna = mm_nt(dmixed, wqkv[...])
        gnm = gn_part[0:tokens, :] + gn_got[...]
        xhat, scale = normalise(rows)
        cot = og2[0:tokens, :].astype(F32)
        input_grad[...] = (
            cot
            + norm_back(gna, xhat, scale, row(again))
            + norm_back(gnm, xhat, scale, row(mgain))
        ).astype(BF16)
        small[0:1, :] = jnp.sum(gna * xhat, axis=0, keepdims=True)
        small[1:2, :] = jnp.sum(gna, axis=0, keepdims=True)
        small[2:3, :] = jnp.sum(gnm * xhat, axis=0, keepdims=True)
        small[3:4, :] = jnp.sum(gnm, axis=0, keepdims=True)
        for k in range(3):
            cols = dmixed[:, k * width : (k + 1) * width].astype(F32)
            small[4 + k : 5 + k, :] = jnp.sum(cols, axis=0, keepdims=True)
        small[7:8, :] = jnp.sum(cot, axis=0, keepdims=True)
        per = half_ff // width
        for side in range(2):
            here = (1 - core if side == 0 else core).astype(F32)
            for k in range(per):
                at = 8 + side * per + k
                small[at : at + 1, :] = bins[0:1, k * width : (k + 1) * width] * here

    rounds = [
        [place.flip(0)],
        [place.flip(1)],
        [place.to_seq()],
        [place.to_rest(by) for by in range(1, n_rest)],
    ]

    def vec_start(r):
        for i, device in enumerate(rounds[r]):
            go("vec" + str(r), small.at[pl.ds(0, small.shape[0])] if r == 0 else small_got.at[8 + r], small_got.at[2 * r if r < 3 else 5 + i], device)

    def vec(r):
        if r == 0:
            vec_start(0)
            return
        arrive("vec" + str(r - 1))
        source = small[...] if r == 1 else small_got[8 + r - 1]
        small_got[8 + r] = source + small_got[2 * (r - 1)]
        vec_start(r)

    def vec_end():
        arrive("vec3")
        total = small_got[8 + 3]
        for i in range(n_rest - 1):
            total = total + small_got[5 + i]
        vec_out[...] = total

    first, second = [], []
    at = 0
    for found, units, data, offset in ((first, units1, grads1, 0), (second, units2, grads2, rows1)):
        for base, size, order in units:
            found.append(Chain(
                place, wires, data, base, size, order, got.at[pl.ds(at, size)], final, offset + base,
                free_sem.at[len(first) + len(second)], keep_sem.at[len(first) + len(second)],
            ))
            at += size

    todo = {"front": front, "part": part, "tail": tail}
    for g in range(3):
        todo["mlp" + str(g)] = functools.partial(mlp_group, g)
    for r in range(4):
        todo["vec" + str(r)] = functools.partial(vec, r)
    runs = {}
    for j in range(PER_GROUP):
        for name, action in (
            ("send", send), ("line", lambda j: arrive("line" + str(j))), ("spread", spread), ("fwd", forward),
            ("keys", keys_there), ("core", core_sum), ("plane", plane_sum), ("home", home), ("grad", grad),
        ):
            todo[name + str(j)] = functools.partial(action, j)
        runs[j] = attend(j)
        todo["a" + str(j)] = functools.partial(next, runs[j])
    for name, units in (("u", first), ("v", second)):
        for i, unit in enumerate(units):
            for stage in range(2 * unit.depth + 1):
                todo[name + str(i) + "." + str(stage)] = functools.partial(unit.stage, stage)
    for j in range(PER_GROUP):
        leaving[j] = []
    for token in SCHEDULE:
        before = len(sent)
        todo[token]()
        if token[:-1] in ("spread", "fwd"):
            leaving[int(token[-1])] += sent[before:]
            del sent[before:]
    vec_end()
    for unit in first + second:
        if unit.sent:
            unit.finish()
    for copy in sent:
        copy.wait_send()


def joined(mesh, positions, hid, og, again, abias, mgain, mbias, bqkv, bdense, bout, b_in, wqkv, wdense, win, wout):
    n_seq, n_blk = mesh.shape["seq"], mesh.shape["blk"]
    n_low, n_rest = n_blk // HEAD_GROUPS, n_blk // 4
    tokens, width = hid.shape
    half_ff = win.shape[1] // 2
    rows1, rows2 = 2 * half_ff, 2 * width
    size = half_ff // 3
    units1 = [(i * size, size, order) for i, order in enumerate(ORDERS[:6])]
    size = rows2 // 6
    units2 = [(i * size, size, order) for i, order in enumerate(ORDERS[6:])]
    total = rows1 + rows2
    copies = 9 * (len(units1) + len(units2)) + 128
    line = (HEAD_GROUPS, tokens, 128)
    n_small = 8 + 2 * half_ff // width
    devices = HEAD_GROUPS * n_low
    per = PER_GROUP
    inputs = [positions, hid, og, again, abias, mgain, mbias, bqkv, bdense, bout, b_in, wqkv, wdense, win, wout]
    return pl.pallas_call(
        functools.partial(joined_kernel, n_seq, n_blk, units1, units2),
        out_shape=[
            jax.ShapeDtypeStruct((tokens, width), BF16),
            jax.ShapeDtypeStruct((tokens, width), BF16),
            jax.ShapeDtypeStruct((n_small, width), F32),
            jax.ShapeDtypeStruct((2, total, width), BF16),
        ],
        in_specs=[IN_SMEM] + [IN_VMEM] * (len(inputs) - 5) + [pl.BlockSpec(memory_space=pl.ANY)] * 4,
        out_specs=[IN_VMEM] * 3 + [pl.BlockSpec(memory_space=pl.ANY)],
        scratch_shapes=[
            pltpu.VMEM(wqkv.shape, BF16),
            pltpu.VMEM(wdense.shape, BF16),
            pltpu.VMEM((2, width, FF_CHUNK), BF16),
            pltpu.VMEM((2, FF_CHUNK, width), BF16),
            pltpu.VMEM((tokens, 2 * HEAD_DIM), F32),
            pltpu.VMEM((tokens, 2 * HEAD_DIM), F32),
            pltpu.VMEM((tokens, 2 * HEAD_DIM), F32),
            pltpu.VMEM((2 * tokens, width), BF16),
            pltpu.VMEM((2 * tokens, width), BF16),
            pltpu.VMEM((2 * tokens, width), BF16),
            pltpu.VMEM((2 * tokens, width), BF16),
            pltpu.VMEM((per,) + line, BF16),
            pltpu.VMEM((per,) + line, BF16),
            pltpu.VMEM((per,) + line, BF16),
            pltpu.VMEM((per, n_low) + line, BF16),
            pltpu.VMEM((n_low, HEAD_GROUPS, 16, 128), BF16),
            *attention_scratch(HEAD_GROUPS, devices),
            pltpu.VMEM((per, 3) + line, BF16),
            pltpu.VMEM((per,) + line, BF16),
            pltpu.VMEM((per,) + line, BF16),
            pltpu.VMEM((2 * tokens, width), F32),
            pltpu.VMEM((2 * tokens, width), F32),
            pltpu.VMEM((tokens, width), F32),
            pltpu.VMEM((tokens, width), F32),
            pltpu.VMEM((per, HEAD_GROUPS, tokens, 256), BF16),
            pltpu.VMEM((per, HEAD_GROUPS // 2, tokens, 256), BF16),
            pltpu.VMEM((1, half_ff), F32),
            pltpu.VMEM((rows1, width), BF16),
            pltpu.VMEM((rows2, width), BF16),
            pltpu.VMEM((total, width), BF16),
            pltpu.VMEM((n_small, width), F32),
            pltpu.VMEM((12, n_small, width), F32),
            pltpu.SemaphoreType.DMA((copies,)),
            pltpu.SemaphoreType.DMA((copies,)),
            pltpu.SemaphoreType.DMA((2,)),
            pltpu.SemaphoreType.DMA((2, 2)),
            pltpu.SemaphoreType.DMA((len(units1) + len(units2),)),
            pltpu.SemaphoreType.REGULAR((len(units1) + len(units2),)),
        ],
        compiler_params=pltpu.CompilerParams(
            vmem_limit_bytes=VMEM_BYTES, collective_id=2, has_side_effects=True
        ),
        name="joined",
    )(*inputs)


def spread_kernel(
    n_blk, positions, final, vec, out_rows, grad_rows,
    output, input_grad, win, wout, wqkv, wdense, again, abias, mgain, mbias, bqkv, bdense, bin_, bout,
):
    half_ff = win.shape[1] // 2

    @pl.when(pl.program_id(0) == 0)
    def _():
        width = vec.shape[1]
        _, turned_rows = runs_of(positions, n_blk)
        cut = (GROUP // 16, 16, 128)
        for src, dst in ((out_rows, output), (grad_rows, input_grad)):
            for at in range(0, width, 128):
                cols = slice(at, at + 128)
                one, two = src[0:GROUP, cols].reshape(cut), src[GROUP : 2 * GROUP, cols].reshape(cut)
                dst[0:GROUP, cols] = jnp.where(turned_rows, two, one).reshape(GROUP, 128)
                dst[GROUP : 2 * GROUP, cols] = jnp.where(turned_rows, one, two).reshape(GROUP, 128)
        for ref, at in ((again, 0), (abias, 1), (mgain, 2), (mbias, 3), (bqkv, 4), (bdense, 7), (bout, 7), (bin_, 8)):
            for k in range(ref.shape[0] // width):
                ref[k * width : (k + 1) * width] = vec[at + k : at + k + 1, :].reshape(width)

    for core in range(2):
        win[:, core * half_ff : (core + 1) * half_ff] = final[core, 0:half_ff, :].T.astype(F32)
        wout[core * half_ff : (core + 1) * half_ff, :] = final[core, half_ff : 2 * half_ff, :].astype(F32)

    def segment(head, part):
        group, j = head // PER_GROUP, head % PER_GROUP
        half = HEAD_GROUPS // 2
        at = 2 * half_ff + (j * half + group % half) * 256 + part * HEAD_DIM
        return final[group // half, at : at + HEAD_DIM, :]

    width = wdense.shape[0]
    for tile in range(HEADS // 2):
        for part in range(4):
            both = jnp.concatenate([segment(2 * tile, part), segment(2 * tile + 1, part)], axis=0)
            if part == 0:
                wdense[tile * 128 : tile * 128 + 128, :] = both.astype(F32)
            else:
                at = (part - 1) * width + tile * 128
                wqkv[:, at : at + 128] = both.T.astype(F32)


def spread_out(n_blk, positions, final, vec, out_rows, grad_rows, ff):
    total, width = final.shape[1:]
    lanes = 128

    def whole(x):
        return pl.BlockSpec(x.shape, lambda i: (0,) * len(x.shape))

    vectors = [jax.ShapeDtypeStruct((n,), F32) for n in (width, width, width, width, 3 * width, width, ff, width)]
    rows = jax.ShapeDtypeStruct(out_rows.shape, BF16)
    return pl.pallas_call(
        functools.partial(spread_kernel, n_blk),
        grid=(width // lanes,),
        in_specs=[IN_SMEM, pl.BlockSpec((2, total, lanes), lambda i: (0, 0, i))]
        + [whole(x) for x in (vec, out_rows, grad_rows)],
        out_specs=[
            whole(rows),
            whole(rows),
            pl.BlockSpec((lanes, ff), lambda i: (i, 0)),
            pl.BlockSpec((ff, lanes), lambda i: (0, i)),
            pl.BlockSpec((lanes, 3 * width), lambda i: (i, 0)),
            pl.BlockSpec((width, lanes), lambda i: (0, i)),
        ]
        + [whole(x) for x in vectors],
        out_shape=[
            rows,
            rows,
            jax.ShapeDtypeStruct((width, ff), F32),
            jax.ShapeDtypeStruct((ff, width), F32),
            jax.ShapeDtypeStruct((width, 3 * width), F32),
            jax.ShapeDtypeStruct((width, width), F32),
        ]
        + vectors,
        compiler_params=params(),
        name="spread",
    )(positions, final, vec, out_rows, grad_rows)


def rotary_tables(positions):
    lane = jnp.arange(128, dtype=jnp.int32) % HEAD_DIM
    half = ROTARY // 2
    inverse = jnp.power(ROTARY_BASE, -2.0 * (lane % half).astype(F32) / ROTARY)
    angles = positions.astype(F32)[:, None] * inverse[None, :]
    cosine, sine = jnp.cos(angles), jnp.sin(angles)
    lane = lane[None, :]
    return (
        jnp.where(lane < ROTARY, cosine, 1.0),
        jnp.where(lane < half, -sine, 0.0),
        jnp.where((lane >= half) & (lane < ROTARY), sine, 0.0),
    )


def solution(mesh):
    n_seq, n_blk = mesh.shape["seq"], mesh.shape["blk"]
    n_low = n_blk // HEAD_GROUPS
    low_bits = n_low.bit_length() - 1
    def permute(x, target):
        return lax.ppermute(x, "blk", [(b, target(b)) for b in range(n_blk)])

    def to_group(x, by):
        return permute(x, lambda b: ((b // n_low + by) % HEAD_GROUPS) * n_low + b % n_low)

    def flip(x, bit):
        return permute(x, lambda b: b ^ (1 << bit))

    def on_device(
        hidden, positions, ln_attn_gain, ln_attn_bias, ln_mlp_gain, ln_mlp_bias,
        w_qkv, b_qkv, w_dense, b_dense, w_in, b_in, w_out, b_out, out_grad,
    ):
        hid, og, pos = hidden[0], out_grad[0], positions[0]
        again, abias = ln_attn_gain[None], ln_attn_bias[None]
        mgain, mbias = ln_mlp_gain[None], ln_mlp_bias[None]
        tokens, width = hid.shape
        if n_low == 4:
            output, input_grad, vec, final = joined(
                mesh, positions, hid, og, ln_attn_gain, ln_attn_bias, ln_mlp_gain, ln_mlp_bias, b_qkv, b_dense, b_out,
                b_in, w_qkv, w_dense, w_in, w_out,
            )
            output, input_grad, win, wout, wqkv, wdense, *vectors = spread_out(
                n_blk, positions, final, vec, output, input_grad, w_in.shape[1]
            )
            dgain, dbias, dmgain, dmbias, dbqkv, dbdense, dbin, dbout = vectors
            return (
                output[None], input_grad[None], dgain, dbias, dmgain, dmbias,
                wqkv, dbqkv, wdense, dbdense, win, dbin, wout, dbout,
            )
        b = lax.axis_index("blk")
        core = b % 2
        hi = b // n_low
        tables = rotary_tables(pos)

        own_runs = pos[::GROUP] // GROUP
        line_runs = jnp.concatenate(
            [own_runs] + [to_group(own_runs, by) for by in range(1, HEAD_GROUPS)]
        )
        key_runs = [line_runs]
        for bit in range(low_bits - 1, -1, -1):
            key_runs = key_runs + [flip(r, bit) for r in key_runs]
        n_query = line_runs.shape[0]
        rank = jnp.sum(line_runs[:, None] > line_runs[None, :], axis=1)
        slots = rank[None, :] == jnp.arange(n_query)[:, None]
        order = jnp.sum(jnp.where(slots, jnp.arange(n_query)[None, :], 0), axis=1)
        ordered = jnp.sum(jnp.where(slots, line_runs[None, :], 0), axis=1)
        tab = jnp.concatenate(key_runs + [order, ordered]).astype(jnp.int32)

        hid2 = jnp.concatenate([hid, flip(hid, 0)], axis=0)
        og2 = jnp.concatenate([og, flip(og, 0)], axis=0)

        msg = front(hid, og, again, abias, w_qkv, b_qkv[None], w_dense, tables)

        arrived = []
        for j in range(PER_GROUP):
            got = []
            for by in range(HEAD_GROUPS):
                part = lax.dynamic_index_in_dim(msg[j], lax.rem(hi + by, HEAD_GROUPS), 0, False)
                got.append(part if by == 0 else to_group(part, by))
            qd = jnp.stack([g[0] for g in got])
            pieces = [jnp.stack([g[1] for g in got])]
            for bit in range(low_bits - 1, -1, -1):
                pieces = pieces + [flip(piece, bit) for piece in pieces]
            arrived.append((qd, pieces))

        mlp_grads, bin_half, out_part, gn_part, normed2 = mlp(
            core[None].astype(jnp.int32), hid2, og2, again, abias, mgain, mbias, w_in, b_in[None], w_out
        )
        odqs, dkvs = [], []
        line = (HEAD_GROUPS, tokens, 128)
        for j in range(PER_GROUP):
            qd, pieces = arrived[j]
            runs = (HEAD_GROUPS * tokens // GROUP, GROUP, 128)
            odq, dkv = attention(tab, qd.reshape(runs), [p.reshape(runs) for p in pieces])
            odqs.append(odq.reshape(line))
            dkvs.append([d.reshape(line) for d in dkv])

        zero = jnp.zeros_like(bin_half)
        bins = jnp.where(
            core == 0, jnp.concatenate([bin_half, zero], 1), jnp.concatenate([zero, bin_half], 1)
        ).reshape(-1, width)
        half_ff = mlp_grads.shape[1]
        output, input_grad, vec, final = finish(
            mesh, odqs, dkvs, mlp_grads.reshape(2 * half_ff, width), out_part, gn_part, hid, og, og2,
            normed2, bins, again, mgain, w_qkv, w_dense, b_dense[None], b_out[None], tables,
        )
        win, wout, wqkv, wdense = expand(
            final, ((half_ff, True), (half_ff, False), (3 * width // 2, True), (width // 2, False))
        )
        return (
            output[None],
            input_grad[None],
            vec[0],
            vec[1],
            vec[2],
            vec[3],
            wqkv,
            vec[4:7].reshape(-1),
            wdense,
            vec[7],
            win,
            vec[8:].reshape(-1),
            wout,
            vec[7],
        )

    rows = P("seq", "blk", None)
    return jax.shard_map(
        on_device,
        mesh=mesh,
        in_specs=(rows, P("seq", "blk")) + (P(),) * 12 + (rows,),
        out_specs=(rows, rows) + (P(),) * 12,
        check_vma=False,
    )
```

profile of v0, /device:TPU:0, one launch (start us, length us, event | category | flops | bytes accessed | tf_op | source)
XLA Modules:
  0.0 183.4 jit_solution(2963793885251899342)
XLA Ops:
  0.7 166.5 %joined.1 = (bf16[256,768]{1,0:T(8,128)(2,1)}, bf16[256,768]{1,0:T(8,128)(2,1)}, f32[12,768]{1,0:T(8,128)}, bf16[2,4608,768]{2,1,0:T(8,128)(2,1)}) custom-call(s32[1,256]{1,0:T(1,128)} %positions.3, bf16[256,768]{1,0:T(8,128)(2,1)} %bitcast.4, bf16[256,768]{1,0:T(8,128)(2,1)} %bitcast.5, bf16[768]{0:T(1024)(128)(2,1)} %again.1, bf16[768]{0:T(1024)(128)(2,1)} %abias.1, ...), custom_call_target="tpu_custom_call" | custom-call | tf_op jit(solution)/shard_map/joined/pallas_call | solution.py:1509
  167.1 16.0 %spread.1 = (bf16[256,768]{1,0:T(8,128)(2,1)}, bf16[256,768]{1,0:T(8,128)(2,1)}, f32[768,3072]{1,0:T(8,128)}, f32[3072,768]{1,0:T(8,128)}, f32[768,2304]{1,0:T(8...) custom-call(s32[1,256]{1,0:T(1,128)} %positions.3, ...), custom_call_target="tpu_custom_call" | custom-call | tf_op jit(solution)/shard_map/spread/pallas_call | solution.py:1617
where the time goes:
time: 187 us; the launch traced here: 183 us
  Pallas kernels  182 us (97%)
    pallas_call x1, Pallas kernels, joined(): pl.pallas_call(functools.partial(joined_kernel, n_seq, n_blk, units1, uni...  166 us
    pallas_call x1, Pallas kernels, spread_out(): pl.pallas_call(functools.partial(spread_kernel, n_blk), grid=(width // la...  16 us

commit v1 on v0

--- a/solution.py
+++ b/solution.py
@@ -1099,20 +1099,20 @@
 
 
 SCHEDULE = (
-    "front", "send0", "mlp0", "u0.0", "u3.0", "mlp1", "mlp2", "u5.0", "send1", "line0", "spread0", "u0.1", "fwd0",
-    "u4.0", "u3.1", "send2", "u5.1", "line1", "spread1", "keys0", "a0", "a0", "u0.2", "u4.1", "u5.2", "a0", "fwd1",
-    "line2", "u3.2", "u0.3", "spread2", "u5.3", "a0", "u4.2", "u2.0", "keys1", "a1", "u5.4", "u3.3", "a1", "u1.0",
-    "fwd2", "a1", "u0.4", "core0", "u5.5", "a1", "u2.1", "u5.6", "u3.4", "keys2", "a2", "u0.5", "core1", "a2",
-    "plane0", "u1.1", "u4.3", "u5.7", "u0.6", "u3.5", "a2", "a2", "u2.2", "home0", "u3.6", "plane1", "u4.4", "u1.2",
-    "core2", "grad0", "u0.7", "v0.1", "plane2", "home1", "u4.5", "u1.3", "grad1", "v0.2", "v1.1", "u2.3", "home2",
-    "u4.6", "part", "u1.4", "v0.3", "v3.1", "v2.1", "u2.4", "grad2", "u1.5", "v0.4", "v3.2", "u4.7", "u1.6", "v0.5",
-    "u3.7", "v2.2", "u2.5", "v3.3", "tail", "v4.1", "v3.4", "v5.1", "v2.3", "v0.6", "u2.6", "v1.2", "vec0", "u1.7",
-    "v3.5", "v2.4", "u0.8", "v1.3", "v1.4", "u4.8", "u2.7", "v4.2", "u3.8", "v1.5", "v5.2", "v3.6", "v0.7", "v2.5",
-    "v4.3", "v5.3", "u5.8", "v5.4", "v1.6", "v2.6", "v4.4", "v3.7", "u1.8", "v5.5", "v4.5", "v4.6", "v5.6", "v2.7",
-    "vec1", "v0.8", "u2.8", "v4.7", "v5.7", "v1.7", "v3.8", "v2.8", "vec2", "v4.8", "v5.8", "vec3", "v1.8",
+    "front", "send0", "mlp0", "u0.0", "u3.0", "mlp1", "send1", "u4.0", "line0", "spread0", "mlp2", "u0.1", "send2",
+    "u3.1", "line1", "fwd0", "spread1", "u5.0", "u2.0", "keys0", "a0", "u1.0", "u3.2", "u4.1", "a0", "a0", "u0.2",
+    "u3.3", "fwd1", "a0", "keys1", "u5.1", "a1", "u0.3", "core0", "u3.4", "line2", "spread2", "u5.2", "u1.1", "u4.2",
+    "a1", "u5.3", "u0.4", "a1", "u3.5", "plane0", "u2.1", "u5.4", "fwd2", "a1", "u3.6", "keys2", "a2", "u1.2", "u4.3",
+    "core1", "u5.5", "u0.5", "home0", "a2", "part", "u3.7", "grad0", "u1.3", "u2.2", "a2", "u4.4", "u5.6", "plane1",
+    "a2", "u4.5", "u0.6", "u2.3", "core2", "u5.7", "u1.4", "v1.1", "home1", "grad1", "u0.7", "v0.1", "plane2", "v0.2",
+    "u2.4", "v3.1", "u4.6", "u1.5", "home2", "v2.1", "v1.2", "u3.8", "v3.2", "grad2", "u2.5", "u5.8", "v1.3", "u4.7",
+    "v3.3", "u0.8", "u1.6", "v2.2", "u2.6", "tail", "v4.1", "v1.4", "v3.4", "u1.7", "v5.1", "vec0", "v2.3", "v1.5",
+    "v0.3", "v3.5", "v4.2", "v5.2", "v2.4", "u2.7", "v0.4", "vec1", "v2.5", "v4.3", "v5.3", "v0.5", "v3.6", "u4.8",
+    "v2.6", "v4.4", "v5.4", "v3.7", "v4.5", "u1.8", "v1.6", "v5.5", "v0.6", "v2.7", "u2.8", "v4.6", "v5.6", "v1.7",
+    "vec2", "v0.7", "v3.8", "v4.7", "v2.8", "v5.7", "vec3", "v1.8", "v0.8", "v5.8", "v4.8",
 )
 FF_CHUNK = 256
-ORDERS = ("yxmf", "yxmf", "xymf", "xymf", "yxmf", "yxmf", "yxmf", "xymf", "yxmf", "xymf", "xymf", "yxmf")
+ORDERS = ("xymf", "xmyf", "yxmf", "yxmf", "ymxf", "yxmf", "ymxf", "xmyf", "yxmf", "xmyf", "yxmf", "xmyf")
 
 
 def runs_of(positions, n_blk):
@@ -1607,7 +1607,7 @@
 
 def spread_out(n_blk, positions, final, vec, out_rows, grad_rows, ff):
     total, width = final.shape[1:]
-    lanes = 128
+    lanes = 384
 
     def whole(x):
         return pl.BlockSpec(x.shape, lambda i: (0,) * len(x.shape))

time: 187 us -> 181 us (0.968)
  Pallas kernels: 182 us -> 177 us
    pallas_call x1, Pallas kernels: 166 us -> 163 us  [joined(): pl.pallas_call(functools.partial(joined_kernel, n_seq, n_blk, units1, uni...]
    pallas_call x1, Pallas kernels: 16 us -> 13.8 us  [spread_out(): pl.pallas_call(functools.partial(spread_kernel, n_blk), grid=(width // la...]
where the time goes in v1:
time: 181 us; the launch traced here: 178 us
  Pallas kernels  177 us (98%)
    pallas_call x1, Pallas kernels, joined(): pl.pallas_call(functools.partial(joined_kernel, n_seq, n_blk, units1, uni...  163 us
    pallas_call x1, Pallas kernels, spread_out(): pl.pallas_call(functools.partial(spread_kernel, n_blk), grid=(width // la...  13.8 us

profile of v1, /device:TPU:0, one launch (start us, length us, event | category | flops | bytes accessed | tf_op | source)
XLA Modules:
  0.0 177.9 jit_solution(4422768320262701126)
XLA Ops:
  0.7 163.2 %joined.1 = (bf16[256,768]{1,0:T(8,128)(2,1)}, bf16[256,768]{1,0:T(8,128)(2,1)}, f32[12,768]{1,0:T(8,128)}, bf16[2,4608,768]{2,1,0:T(8,128)(2,1)}) custom-call(s32[1,256]{1,0:T(1,128)} %positions.3, bf16[256,768]{1,0:T(8,128)(2,1)} %bitcast.4, bf16[256,768]{1,0:T(8,128)(2,1)} %bitcast.5, bf16[768]{0:T(1024)(128)(2,1)} %again.1, bf16[768]{0:T(1024)(128)(2,1)} %abias.1, ...), custom_call_target="tpu_custom_call" | custom-call | tf_op jit(solution)/shard_map/joined/pallas_call | solution.py:1509
  163.8 13.8 %spread.1 = (bf16[256,768]{1,0:T(8,128)(2,1)}, bf16[256,768]{1,0:T(8,128)(2,1)}, f32[768,3072]{1,0:T(8,128)}, f32[3072,768]{1,0:T(8,128)}, f32[768,2304]{1,0:T(8...) custom-call(s32[1,256]{1,0:T(1,128)} %positions.3, ...), custom_call_target="tpu_custom_call" | custom-call | tf_op jit(solution)/shard_map/spread/pallas_call | solution.py:1617

commit v2 on v1

--- a/solution.py
+++ b/solution.py
@@ -1050,7 +1050,14 @@
             kept = pl.ds(pl.multiple_of(self.bases[-1], 16), half)
             self.up.append(wires.copy(data.at[kept], data.at[kept], device))
         whole = pl.ds(base, size)
-        self.up.insert(0, wires.copy(data.at[whole], final.at[place.core, pl.ds(final_base, size)], place.flip(0)))
+
+        def across(start):
+            rows = pl.ds(pl.multiple_of(start, 16), size // 2)
+            there = pl.ds(pl.multiple_of(start + final_base - base, 16), size // 2)
+            return wires.copy(data.at[rows], final.at[place.core, there], place.flip(0))
+
+        self.near = across(self.bases[1])
+        self.up.insert(0, across(base + (1 - self.bits[0]) * (size // 2)))
         self.depth = len(order)
         self.keep = pltpu.make_async_copy(data.at[whole], final.at[place.core, pl.ds(final_base, size)], keep)
         self.free, self.first = free, pairs[order[0]][1]
@@ -1088,10 +1095,13 @@
             if level == 2:
                 pl.semaphore_wait(self.free, 1)
             self.start(self.up[level - 1])
+            if level == 2:
+                self.start(self.near)
             if level == 1:
                 self.keep.start()
 
     def finish(self):
+        self.near.wait_recv()
         self.up[0].wait_recv()
         self.keep.wait()
         for copy in self.sent:
@@ -1500,7 +1510,7 @@
     size = rows2 // 6
     units2 = [(i * size, size, order) for i, order in enumerate(ORDERS[6:])]
     total = rows1 + rows2
-    copies = 9 * (len(units1) + len(units2)) + 128
+    copies = 10 * (len(units1) + len(units2)) + 128
     line = (HEAD_GROUPS, tokens, 128)
     n_small = 8 + 2 * half_ff // width
     devices = HEAD_GROUPS * n_low

time: 181 us -> 181 us (level)
  no operation moved by 1% of the time
where the time goes in v2:
time: 181 us; the launch traced here: 177 us
  Pallas kernels  176 us (97%)
    pallas_call x1, Pallas kernels, joined(): pl.pallas_call(functools.partial(joined_kernel, n_seq, n_blk, units1, uni...  163 us
    pallas_call x1, Pallas kernels, spread_out(): pl.pallas_call(functools.partial(spread_kernel, n_blk), grid=(width // la...  13.8 us

profile of v2, /device:TPU:0, one launch (start us, length us, event | category | flops | bytes accessed | tf_op | source)
XLA Modules:
  0.0 177.4 jit_solution(10887841867101259438)
XLA Ops:
  0.7 162.7 %joined.1 = (bf16[256,768]{1,0:T(8,128)(2,1)}, bf16[256,768]{1,0:T(8,128)(2,1)}, f32[12,768]{1,0:T(8,128)}, bf16[2,4608,768]{2,1,0:T(8,128)(2,1)}) custom-call(s32[1,256]{1,0:T(1,128)} %positions.3, bf16[256,768]{1,0:T(8,128)(2,1)} %bitcast.4, bf16[256,768]{1,0:T(8,128)(2,1)} %bitcast.5, bf16[768]{0:T(1024)(128)(2,1)} %again.1, bf16[768]{0:T(1024)(128)(2,1)} %abias.1, ...), custom_call_target="tpu_custom_call" | custom-call | tf_op jit(solution)/shard_map/joined/pallas_call | solution.py:1519
  163.3 13.8 %spread.1 = (bf16[256,768]{1,0:T(8,128)(2,1)}, bf16[256,768]{1,0:T(8,128)(2,1)}, f32[768,3072]{1,0:T(8,128)}, f32[3072,768]{1,0:T(8,128)}, f32[768,2304]{1,0:T(8...) custom-call(s32[1,256]{1,0:T(1,128)} %positions.3, ...), custom_call_target="tpu_custom_call" | custom-call | tf_op jit(solution)/shard_map/spread/pallas_call | solution.py:1627
